TPU v7x, 32 devices: a whole 2x2x4 slice. The times are simulated.
32 devices in a mesh: grp: 4 (over y, x), dev: 8 (over z, core).
Axes of the slice: x: 2, y: 2, z: 4, core: 2. Of those that a mesh axis runs over, the one named last changes fastest.
Arguments:
- field: float32 [512, 512, 256, 4], P('dev', 'grp'), may hold values from -21 to 21
- start_basis: float32 [512, 64], replicated, may hold values from -6 to 6
Outputs:
- factor: float32 [512, 64], replicated
- core: float32 [64, 512, 256, 4], P(None, ('grp', 'dev'))
All inputs are finite; a program needn't handle non-finite values.
Results may differ from a plain program's by a relative error of at most 0.0003.
Values sent between devices are 32-bit elements; how exact they have to be, the bound alone decides.
A program may use at most 192 MiB of HBM per device.

v0:
```python
import jax
import jax.numpy as jnp
from jax import lax
from jax.sharding import PartitionSpec as P

ITERS = 3


def product(left, right):
    return jnp.dot(left, right, precision=lax.Precision.HIGHEST, preferred_element_type=jnp.float32)


def on_device(field, start_basis):
    regrouped = lax.all_to_all(field, "dev", split_axis=1, concat_axis=0, tiled=True)
    rows = regrouped.shape[0]
    local_cols = regrouped.shape[1] * regrouped.shape[2] * regrouped.shape[3]
    unfold = regrouped.reshape(rows, local_cols)
    local_gram = product(unfold, unfold.T)
    gram = lax.psum(local_gram, ("grp", "dev"))
    basis = start_basis
    for step in range(ITERS):
        image = product(gram, basis)
        cross = product(image.T, image)
        chol = jnp.linalg.cholesky(cross)
        basis = lax.linalg.triangular_solve(
            chol, image, left_side=False, lower=True, transpose_a=True
        )
    core = product(basis.T, unfold)
    return (
        basis,
        core.reshape(basis.shape[1], regrouped.shape[1], regrouped.shape[2], regrouped.shape[3]),
    )


def solution(mesh):
    placed = (P("dev", "grp", None, None), P())
    return jax.shard_map(
        on_device,
        mesh=mesh,
        in_specs=placed,
        out_specs=(P(), P(None, ("grp", "dev"), None, None)),
        check_vma=False,
    )
```

profile of v0, /device:TPU:0, one launch (start us, length us, event | category | flops | bytes accessed | tf_op | source)
XLA Modules:
  0.0 1174.3 jit_solution(12790199668658343280)
XLA Ops:
  7.2 22.6 %copy.14 = f32[64,128,256,4]{2,3,0,1:T(4,128)} copy(f32[64,128,256,4]{2,3,1,0:T(4,128)} %param.5) | data formatting | bytes 67108864 | tf_op args[0]
  29.8 735.1 %all_to_all.15 = f32[64,128,256,4]{2,3,0,1:T(4,128)} all-to-all(f32[64,128,256,4]{2,3,0,1:T(4,128)} %copy.14), channel_id=1, replica_groups=mesh['grp'=4,'dev'=8] {'dev'}, dimensions={1} | all-to-all | bytes 67108864 | tf_op jit(solution)/shard_map/all_to_all | solution.py:14
  764.9 59.0 %copy.15 = f32[64,8,16,256,4]{0,1,4,3,2:T(8,128)} copy(f32[64,8,16,256,4]{3,4,0,2,1:T(4,128)} %bitcast.63) | data formatting | bytes 67108864 | tf_op jit(solution)/shard_map/all_to_all | solution.py:14
  823.9 54.6 %reshape.21 = f32[512,16384]{0,1:T(8,128)} reshape(f32[8,64,16,256,4]{1,0,4,3,2:T(8,128)} %bitcast.1) | data formatting | bytes 67108864 | tf_op jit(solution)/shard_map/reshape | solution.py:17
  878.4 60.9 %fusion.17 = f32[512,512]{1,0:T(8,128)} fusion(f32[512,16384]{0,1:T(8,128)} %reshape.21), kind=kOutput, calls=%fused_computation.31 | convolution fusion | flops 51539607552 | bytes 34603008 | tf_op jit(solution)/shard_map/dot_general | solution.py:10
  939.4 37.5 %dot_general.36 = f32[16,256,4,512]{3,2,1,0:T(4,128)} reshape(f32[16384,512]{1,0:T(8,128)} %bitcast.62) | data formatting | bytes 67108864 | tf_op jit(solution)/shard_map/dot_general | solution.py:10
  976.9 93.0 %all-reduce.2.cloned.1.call-done = f32[512,512]{1,0:T(8,128)} async-done(((f32[512,512]{1,0:T(8,128)}), f32[512,512]{1,0:T(8,128)}) %all-reduce.2.cloned.1.call-update) | async-done | bytes 1048592 | tf_op jit(solution)/shard_map/psum | solution.py:19
  1069.9 2.4 fusion.18
  1072.6 5.8 cholesky.59
  1078.5 0.6 compare_reduce_fusion.2
  1079.1 0.7 fusion.3
  1079.8 4.9 custom-call.7
  1085.0 2.4 fusion.20
  1087.7 5.8 cholesky.70
  1093.6 0.6 compare_reduce_fusion.1
  1094.3 0.7 fusion.4
  1094.9 4.9 custom-call.8
  1100.2 2.4 fusion.22
  1102.9 5.8 cholesky.81
  1108.8 0.6 compare_reduce_fusion
  1109.4 0.7 fusion.5
  1110.1 4.9 custom-call.9
  1115.3 45.2 %fusion = f32[64,16,256,4]{2,0,3,1:T(8,128)} fusion(f32[16,256,4,512]{3,2,1,0:T(4,128)} %dot_general.36, f32[64,512]{1,0:T(8,128)S(1)} %fusion.6), kind=kOutput, calls=%fused_computation | convolution fusion | flops 6442450944 | bytes 37879808 | tf_op jit(solution)/shard_map/dot_general | solution.py:10
  1160.5 6.9 copy.20
  (21 shorter events, 2.2 us)
Async XLA Ops:
  7.2 1062.7 %copy-start = (f32[512,64]{0,1:T(8,128)S(1)}, f32[512,64]{0,1:T(8,128)}, u32[]{:S(2)}) copy-start(f32[512,64]{0,1:T(8,128)} %param.6) | copy-start | bytes 393220
  7.2 1062.7 %all-reduce.2.cloned.1.call-start = ((), (), s32[]{:S(2)}) async-start(), calls=%async_computation.1 | async-start | bytes 2097152 | tf_op jit(solution)/shard_map/psum | solution.py:19
  1115.3 52.1 %copy-start.1 = (f32[64,512]{1,0:T(8,128)}, f32[64,512]{1,0:T(8,128)S(1)}, u32[]{:S(2)}) copy-start(f32[64,512]{1,0:T(8,128)S(1)} %fusion.6) | copy-start | bytes 393220
Sparse Core Ops, SparseCore 0:
  939.5 130.3 all-reduce.1
where the time goes:
time: 1180 us; the launch traced here: 1170 us
  blocking collectives  735 us (62%)
  local copies, waits for them, and re-layouts  181 us (15%)
  matrix products  115 us (10%)
  waiting for transfers between devices  93 us (8%)
  other arithmetic  36.2 us (3%)
  between operations  14.2 us (1%)
    all_to_all x1, blocking collectives, on_device(): lax.all_to_all(field, 'dev', split_axis=1, concat_axis=0, tiled=True)  735 us
    dot_general x8, matrix products, product(): jnp.dot(left, right, precision=lax.Precision.HIGHEST, preferred_element_t...  114 us
    psum x1, waiting for transfers between devices, on_device(): gram = lax.psum(local_gram, ('grp', 'dev'))  93 us
    all_to_all x1, local copies, waits for them, and re-layouts, on_device(): lax.all_to_all(field, 'dev', split_axis=1, concat_axis=0, tiled=True)  59 us
    reshape x1, local copies, waits for them, and re-layouts, on_device(): unfold = regrouped.reshape(rows, local_cols)  54.6 us
    dot_general x4, local copies, waits for them, and re-layouts, product(): jnp.dot(left, right, precision=lax.Precision.HIGHEST, preferred_element_t...  37.7 us
    unnamed x6, local copies, waits for them, and re-layouts  29.5 us
  transfers between devices with their start and end apart: 1, of which 1 were waited for; matrix products, arithmetic and copies ran while one was open for 3% of the time, Pallas kernels for 0%

commit v1 on v0

v1 whole, which is shorter than its diff:
```python
import functools

import jax
import jax.numpy as jnp
from jax import lax
from jax.experimental import pallas as pl
from jax.experimental.pallas import tpu as pltpu
from jax.sharding import PartitionSpec as P

ITERS = 3
LANES = 128
WINDOW = 3
MESH = pl.DeviceIdType.MESH
NT = (((1,), (1,)), ((), ()))


def partner(me, k):
    out, bit = me, 1
    while bit <= k:
        if k & bit:
            out = out + bit * (1 - 2 * ((me // bit) % 2))
        bit *= 2
    return out


def split(x):
    hi = x.astype(jnp.bfloat16)
    return hi, (x - hi.astype(jnp.float32)).astype(jnp.bfloat16)


def exchange_kernel(
    n, field, part, hi_out, lo_out, buf, hi, lo, send_sem, recv_sem, own_sem, flush_sem
):
    chunks, sub = buf.shape[0], buf.shape[2]
    rows = field.shape[0]
    me = lax.axis_index("dev")

    barrier = pltpu.get_barrier_semaphore()
    for k in range(1, n):
        pl.semaphore_signal(
            barrier, inc=1, device_id={"dev": partner(me, k)}, device_id_type=MESH
        )
    pl.semaphore_wait(barrier, n - 1)

    def remote(c, k, column_owner, row_owner):
        return pltpu.make_async_remote_copy(
            src_ref=field.at[:, column_owner * chunks + c],
            dst_ref=buf.at[c, pl.ds(row_owner * rows, rows)],
            send_sem=send_sem.at[c, k - 1],
            recv_sem=recv_sem.at[c, k - 1],
            device_id={"dev": partner(me, k)},
            device_id_type=MESH,
        )

    def own(c):
        return pltpu.make_async_copy(
            field.at[:, me * chunks + c], buf.at[c, pl.ds(me * rows, rows)], own_sem.at[c]
        )

    def start(c):
        for k in range(n - 1, 0, -1):
            remote(c, k, partner(me, k), me).start()
        own(c).start()

    def flush(c, slot):
        return (
            pltpu.make_async_copy(hi.at[slot], hi_out.at[c], flush_sem.at[0, slot]),
            pltpu.make_async_copy(lo.at[slot], lo_out.at[c], flush_sem.at[1, slot]),
        )

    for c in range(min(WINDOW, chunks)):
        start(c)
    part[...] = jnp.zeros_like(part)

    def step(c, carry):
        slot = c % 2
        for k in range(n - 1, 0, -1):
            remote(c, k, partner(me, k), me).wait_send()

        @pl.when(c + WINDOW < chunks)
        def _():
            start(c + WINDOW)

        @pl.when(c >= 2)
        def _():
            for copy in flush(c - 2, slot):
                copy.wait()

        own(c).wait()
        for k in range(1, n):
            remote(c, k, me, partner(me, k)).wait_recv()
        for s in range(sub):
            high, low = split(buf[c, :, s, :])
            hi[slot, :, s * LANES : (s + 1) * LANES] = high
            lo[slot, :, s * LANES : (s + 1) * LANES] = low
        for copy in flush(c, slot):
            copy.start()
        high = hi[slot]
        part[...] += 0.5 * lax.dot_general(
            high, high, NT, preferred_element_type=jnp.float32
        ) + lax.dot_general(high, lo[slot], NT, preferred_element_type=jnp.float32)
        return carry

    lax.fori_loop(0, chunks, step, 0)
    for c in range(max(chunks - 2, 0), chunks):
        for copy in flush(c, c % 2):
            copy.wait()


def exchange(field, n):
    rows, seconds, sub, lanes = field.shape
    chunks, full = seconds // n, rows * n
    wide = sub * lanes
    anywhere = pl.BlockSpec(memory_space=pl.ANY)
    return pl.pallas_call(
        functools.partial(exchange_kernel, n),
        out_shape=(
            jax.ShapeDtypeStruct((full, full), jnp.float32),
            jax.ShapeDtypeStruct((chunks, full, wide), jnp.bfloat16),
            jax.ShapeDtypeStruct((chunks, full, wide), jnp.bfloat16),
        ),
        in_specs=[anywhere],
        out_specs=(pl.BlockSpec(memory_space=pltpu.VMEM), anywhere, anywhere),
        scratch_shapes=[
            pltpu.VMEM((chunks, full, sub, lanes), jnp.float32),
            pltpu.VMEM((2, full, wide), jnp.bfloat16),
            pltpu.VMEM((2, full, wide), jnp.bfloat16),
            pltpu.SemaphoreType.DMA((chunks, n - 1)),
            pltpu.SemaphoreType.DMA((chunks, n - 1)),
            pltpu.SemaphoreType.DMA((chunks,)),
            pltpu.SemaphoreType.DMA((2, 2)),
        ],
        compiler_params=pltpu.CompilerParams(
            collective_id=0, has_side_effects=True, vmem_limit_bytes=56 * 2**20
        ),
    )(field)


def exact(left, right, dims=(((1,), (0,)), ((), ()))):
    return lax.dot_general(
        left, right, dims, precision=lax.Precision.HIGHEST, preferred_element_type=jnp.float32
    )


def inverse_cholesky(cross):
    rank = cross.shape[0]
    row = lax.broadcasted_iota(jnp.int32, (rank, 1), 0)
    here = lax.broadcasted_iota(jnp.int32, (rank, rank), 0)
    there = lax.broadcasted_iota(jnp.int32, (rank, rank), 1)
    left, right = cross, (here == there).astype(jnp.float32)
    for k in range(rank - 1):
        factor = left[:, k : k + 1] / left[k : k + 1, k : k + 1]
        factor = jnp.where(row > k, factor, 0.0)
        left = left - factor * left[k : k + 1, :]
        right = right - factor * right[k : k + 1, :]
    pivots = jnp.sum(jnp.where(here == there, left, 0.0), axis=1, keepdims=True)
    return right / jnp.sqrt(pivots)


def iterate_kernel(part, start, out):
    half = part[...]
    gram = half + half.T
    basis = start[...]
    for _ in range(ITERS):
        image = exact(basis, gram)
        cross = exact(image, image, NT)
        basis = exact(inverse_cholesky(cross), image)
    out[...] = basis


def core_kernel(basis, hi, lo, out):
    sub = out.shape[2]
    rank = basis.shape[0]
    high, low = split(basis[...])
    both = jnp.concatenate([high, low], axis=0)
    first = jnp.dot(both, hi[0], preferred_element_type=jnp.float32)
    second = jnp.dot(high, lo[0], preferred_element_type=jnp.float32)
    result = first[:rank] + first[rank:] + second
    for s in range(sub):
        out[:, 0, s, :] = result[:, s * LANES : (s + 1) * LANES]


def project(basis, hi, lo, sub):
    chunks, full, wide = hi.shape
    rank = basis.shape[0]
    block = pl.BlockSpec((1, full, wide), lambda c: (c, 0, 0))
    return pl.pallas_call(
        core_kernel,
        grid=(chunks,),
        out_shape=jax.ShapeDtypeStruct((rank, chunks, sub, LANES), jnp.float32),
        in_specs=[pl.BlockSpec((rank, full), lambda c: (0, 0)), block, block],
        out_specs=pl.BlockSpec((rank, 1, sub, LANES), lambda c: (0, c, 0, 0)),
        compiler_params=pltpu.CompilerParams(vmem_limit_bytes=40 * 2**20),
    )(basis, hi, lo)


def on_device(field, start_basis):
    n = lax.axis_size("dev")
    rows, seconds, third, fourth = field.shape
    rank = start_basis.shape[1]
    fold = third // LANES
    sub = fold * fourth
    tiles = field.reshape(rows, seconds, fold, LANES, fourth).transpose(0, 1, 2, 4, 3)
    part, hi, lo = exchange(tiles.reshape(rows, seconds, sub, LANES), n)
    part = lax.psum(part, ("grp", "dev"))
    basis = pl.pallas_call(
        iterate_kernel,
        out_shape=jax.ShapeDtypeStruct((rank, start_basis.shape[0]), jnp.float32),
        compiler_params=pltpu.CompilerParams(vmem_limit_bytes=40 * 2**20),
    )(part, start_basis.T)
    core = project(basis, hi, lo, sub)
    core = core.reshape(rank, seconds // n, fold, fourth, LANES).transpose(0, 1, 2, 4, 3)
    return basis.T, core.reshape(rank, seconds // n, third, fourth)


def solution(mesh):
    placed = (P("dev", "grp", None, None), P())
    return jax.shard_map(
        on_device,
        mesh=mesh,
        in_specs=placed,
        out_specs=(P(), P(None, ("grp", "dev"), None, None)),
        check_vma=False,
    )
```

time: 1180 us -> 922 us (0.78)
  Pallas kernels: 0 us -> 776 us
  blocking collectives: 735 us -> 0 us
  local copies, waits for them, and re-layouts: 181 us -> 2.13 us
  matrix products: 115 us -> 0 us
  waiting for transfers between devices: 93 us -> 130 us
  other arithmetic: 36.2 us -> 0 us
    pallas_call x0 -> x3, Pallas kernels: none -> 776 us  [the longest x1 736 us: exchange(): pl.pallas_call(functools.partial(exchange_kernel, n), out_shape=(jax.Shap...]
    all_to_all x1 -> x0, blocking collectives: 735 us -> none  [on_device(): lax.all_to_all(field, 'dev', split_axis=1, concat_axis=0, tiled=True)]
    dot_general x8 -> x0, matrix products: 114 us -> none  [product(): jnp.dot(left, right, precision=lax.Precision.HIGHEST, preferred_element_t...]
    all_to_all x1 -> x0, local copies, waits for them, and re-layouts: 59 us -> none  [on_device(): lax.all_to_all(field, 'dev', split_axis=1, concat_axis=0, tiled=True)]
    reshape x1 -> x0, local copies, waits for them, and re-layouts: 54.6 us -> none  [on_device(): unfold = regrouped.reshape(rows, local_cols)]
    dot_general x4 -> x0, local copies, waits for them, and re-layouts: 37.7 us -> none  [product(): jnp.dot(left, right, precision=lax.Precision.HIGHEST, preferred_element_t...]
    psum x1, waiting for transfers between devices: 93 us -> 130 us  [on_device(): part = lax.psum(part, ('grp', 'dev'))]
    another operation x15 -> x0, other arithmetic: 36.2 us -> none  [the longest x9 19.6 us: on_device(): chol = jnp.linalg.cholesky(cross)]
  transfers between devices with their start and end apart: 1 -> 1, of which waited for: 1 -> 1; matrix products, arithmetic and copies ran while one was open for 3% -> 0% of each run, Pallas kernels for 0% -> 0%
where the time goes in v1:
time: 922 us
  Pallas kernels  776 us (84%)
  waiting for transfers between devices  130 us (14%)
  between operations  14 us (2%)
    pallas_call x1, Pallas kernels, exchange(): pl.pallas_call(functools.partial(exchange_kernel, n), out_shape=(jax.Shap...  736 us
    psum x1, waiting for transfers between devices, on_device(): part = lax.psum(part, ('grp', 'dev'))  130 us
    pallas_call x1, Pallas kernels, on_device(): pl.pallas_call(iterate_kernel, out_shape=jax.ShapeDtypeStruct((rank, star...  20 us
    pallas_call x1, Pallas kernels, project(): pl.pallas_call(core_kernel, grid=(chunks,), out_shape=jax.ShapeDtypeStruc...  19.7 us
  transfers between devices with their start and end apart: 1, of which 1 were waited for; matrix products, arithmetic and copies ran while one was open for 0% of the time, Pallas kernels for 0%

profile of v1, /device:TPU:0, one launch (start us, length us, event | category | flops | bytes accessed | tf_op | source)
XLA Modules:
  0.0 922.0 jit_solution(821930827597693625)
XLA Ops:
  7.2 0.0 all-reduce.2.cloned.1.call-start
  7.2 0.0 copy-start.2
  7.2 736.0 %shard_map.41 = (f32[512,512]{1,0:T(8,128)}, bf16[16,512,1024]{2,1,0:T(8,128)(2,1)}, bf16[16,512,1024]{2,1,0:T(8,128)(2,1)}) custom-call(f32[64,128,8,128]{3,2,1,0:T(8,128)} %bitcast.14), custom_call_target="tpu_custom_call" | custom-call | tf_op jit(solution)/shard_map/pallas_call | solution.py:115
  743.2 0.0 all-reduce.2.cloned.1.call-update
  743.2 130.2 %all-reduce.2.cloned.1.call-done.part = f32[512,512]{1,0:T(8,128)} async-done(((f32[512,512]{1,0:T(8,128)}), f32[512,512]{1,0:T(8,128)}) %all-reduce.2.cloned.1.call-update) | async-done | bytes 1048592 | tf_op jit(solution)/shard_map/psum | solution.py:205
  873.4 0.0 copy-done.2
  873.4 0.0 copy-start
  873.4 1.2 copy-done
  874.6 20.0 %shard_map.42.basis = f32[64,512]{1,0:T(8,128)} custom-call(f32[512,512]{1,0:T(8,128)S(1)} %copy-done, f32[64,512]{1,0:T(8,128)S(1)} %bitcast.13), custom_call_target="tpu_custom_call" | custom-call | tf_op jit(solution)/shard_map/pallas_call | solution.py:206
  894.6 0.0 copy-start.1
  894.6 0.9 copy-done.1
  895.5 19.7 %shard_map.43 = f32[64,16,8,128]{3,2,1,0:T(8,128)} custom-call(f32[64,512]{1,0:T(8,128)S(1)} %copy-done.1, bf16[16,512,1024]{2,1,0:T(8,128)(2,1)} %get-tuple-element.6.hi, bf16[16,512,1024]{2,1,0:T(8,128)(2,1)} %get-tuple-element.7.lo), custom_call_target="tpu_custom_call" | custom-call | tf_op jit(solution)/shard_map/pallas_call | solution.py:187
Async XLA Ops:
  7.2 866.2 %all-reduce.2.cloned.1.call-start = ((), (), s32[]{:S(2)}) async-start(), calls=%async_computation | async-start | bytes 2097152 | tf_op jit(solution)/shard_map/psum | solution.py:205
  7.2 866.2 %copy-start.2 = (f32[512,64]{0,1:T(8,128)S(1)}, f32[512,64]{0,1:T(8,128)}, u32[]{:S(2)}) copy-start(f32[512,64]{0,1:T(8,128)} %param.3) | copy-start | bytes 393220
  873.4 1.2 copy-start
  894.6 0.9 copy-start.1
Sparse Core Ops, SparseCore 0:
  743.3 130.0 all-reduce.1

commit v2 on v1

--- a/solution.py
+++ b/solution.py
@@ -28,19 +28,83 @@
     return hi, (x - hi.astype(jnp.float32)).astype(jnp.bfloat16)
 
 
+def tile_index(i, j):
+    return i * (i + 1) // 2 + j
+
+
+def sum_kernel_stages(n, groups, acc, total, sums, landed, sem):
+    me, grp = lax.axis_index("dev"), lax.axis_index("grp")
+    core, chip, chips = me % 2, me // 2, n // 2
+    half = acc.shape[0] // 2
+    slab = half // groups
+    piece = slab // chips
+    used = [0]
+
+    def send(src, dst, device_id):
+        i = used[0]
+        used[0] += 1
+        copy = pltpu.make_async_remote_copy(
+            src_ref=src, dst_ref=dst, send_sem=sem.at[0, i], recv_sem=sem.at[1, i],
+            device_id=device_id, device_id_type=MESH,
+        )
+        copy.start()
+        return copy
+
+    def finish(copies):
+        for copy in copies:
+            copy.wait()
+
+    pair = {"dev": me + 1 - 2 * core}
+    others = [(grp + k) % groups for k in range(1, groups)]
+    along = [(chip + k) % chips for k in range(1, chips)]
+    pair_sum, grp_sum = sums
+    pair_in, grp_in, chip_in = landed
+
+    finish([send(acc.at[pl.ds((1 - core) * half, half)], pair_in, pair)])
+    pair_sum[...] = acc[pl.ds(core * half, half)] + pair_in[...]
+    finish([
+        send(pair_sum.at[pl.ds(p * slab, slab)], grp_in.at[k], {"grp": p})
+        for k, p in enumerate(others)
+    ])
+    value = pair_sum[pl.ds(grp * slab, slab)]
+    for k in range(groups - 1):
+        value = value + grp_in[k]
+    grp_sum[...] = value
+    finish([
+        send(grp_sum.at[pl.ds(p * piece, piece)], chip_in.at[k], {"dev": p * 2 + core})
+        for k, p in enumerate(along)
+    ])
+    value = grp_sum[pl.ds(chip * piece, piece)]
+    for k in range(chips - 1):
+        value = value + chip_in[k]
+    base = core * half + grp * slab
+    mine = pl.ds(base + chip * piece, piece)
+    total[mine] = value
+    finish([send(total.at[mine], total.at[mine], {"dev": p * 2 + core}) for p in along])
+    mine = pl.ds(base, slab)
+    finish([send(total.at[mine], total.at[mine], {"grp": p}) for p in others])
+    mine = pl.ds(core * half, half)
+    finish([send(total.at[mine], total.at[mine], pair)])
+
+
 def exchange_kernel(
-    n, field, part, hi_out, lo_out, buf, hi, lo, send_sem, recv_sem, own_sem, flush_sem
+    n, groups, field, part, hi_out, lo_out, buf, hi, lo, acc, total, pair_sum, grp_sum,
+    pair_in, grp_in, chip_in, send_sem, recv_sem, own_sem, flush_sem, sum_sem,
 ):
-    chunks, sub = buf.shape[0], buf.shape[2]
+    chunks, full, sub = buf.shape[:3]
     rows = field.shape[0]
-    me = lax.axis_index("dev")
+    me, grp = lax.axis_index("dev"), lax.axis_index("grp")
 
     barrier = pltpu.get_barrier_semaphore()
     for k in range(1, n):
         pl.semaphore_signal(
             barrier, inc=1, device_id={"dev": partner(me, k)}, device_id_type=MESH
         )
-    pl.semaphore_wait(barrier, n - 1)
+    for k in range(1, groups):
+        pl.semaphore_signal(
+            barrier, inc=1, device_id={"grp": (grp + k) % groups}, device_id_type=MESH
+        )
+    pl.semaphore_wait(barrier, n - 1 + groups - 1)
 
     def remote(c, k, column_owner, row_owner):
         return pltpu.make_async_remote_copy(
@@ -70,7 +134,7 @@
 
     for c in range(min(WINDOW, chunks)):
         start(c)
-    part[...] = jnp.zeros_like(part)
+    acc[...] = jnp.zeros_like(acc)
 
     def step(c, carry):
         slot = c % 2
@@ -95,27 +159,51 @@
             lo[slot, :, s * LANES : (s + 1) * LANES] = low
         for copy in flush(c, slot):
             copy.start()
-        high = hi[slot]
-        part[...] += 0.5 * lax.dot_general(
-            high, high, NT, preferred_element_type=jnp.float32
-        ) + lax.dot_general(high, lo[slot], NT, preferred_element_type=jnp.float32)
+        step_rows = 2 * LANES
+        for top in range(0, full, step_rows):
+            own_rows, upto = pl.ds(top, step_rows), pl.ds(0, top + step_rows)
+            high, all_high = hi[slot, own_rows], hi[slot, upto]
+            block = lax.dot_general(high, all_high, NT, preferred_element_type=jnp.float32)
+            block += lax.dot_general(
+                lo[slot, own_rows], all_high, NT, preferred_element_type=jnp.float32
+            )
+            block += lax.dot_general(
+                high, lo[slot, upto], NT, preferred_element_type=jnp.float32
+            )
+            for i in range(top // LANES, (top + step_rows) // LANES):
+                for j in range(i + 1):
+                    at = i * LANES - top
+                    acc[pl.ds(tile_index(i, j) * LANES, LANES)] += block[
+                        at : at + LANES, j * LANES : (j + 1) * LANES
+                    ]
         return carry
 
     lax.fori_loop(0, chunks, step, 0)
     for c in range(max(chunks - 2, 0), chunks):
         for copy in flush(c, c % 2):
             copy.wait()
-
-
-def exchange(field, n):
+    sum_kernel_stages(
+        n, groups, acc, total, (pair_sum, grp_sum), (pair_in, grp_in, chip_in), sum_sem
+    )
+    part[...] = total[...]
+
+
+def exchange(field, n, groups):
     rows, seconds, sub, lanes = field.shape
     chunks, full = seconds // n, rows * n
     wide = sub * lanes
+    chips = n // 2
+    unit = 8 * 2 * groups * chips
+    tiles = full // LANES
+    packed = -(-tile_index(tiles, 0) * LANES // unit) * unit
+    half = packed // 2
+    slab = half // groups
+    stages = 2 * (1 + groups - 1 + chips - 1)
     anywhere = pl.BlockSpec(memory_space=pl.ANY)
     return pl.pallas_call(
-        functools.partial(exchange_kernel, n),
+        functools.partial(exchange_kernel, n, groups),
         out_shape=(
-            jax.ShapeDtypeStruct((full, full), jnp.float32),
+            jax.ShapeDtypeStruct((packed, LANES), jnp.float32),
             jax.ShapeDtypeStruct((chunks, full, wide), jnp.bfloat16),
             jax.ShapeDtypeStruct((chunks, full, wide), jnp.bfloat16),
         ),
@@ -125,10 +213,18 @@
             pltpu.VMEM((chunks, full, sub, lanes), jnp.float32),
             pltpu.VMEM((2, full, wide), jnp.bfloat16),
             pltpu.VMEM((2, full, wide), jnp.bfloat16),
+            pltpu.VMEM((packed, LANES), jnp.float32),
+            pltpu.VMEM((packed, LANES), jnp.float32),
+            pltpu.VMEM((half, LANES), jnp.float32),
+            pltpu.VMEM((slab, LANES), jnp.float32),
+            pltpu.VMEM((half, LANES), jnp.float32),
+            pltpu.VMEM((groups - 1, slab, LANES), jnp.float32),
+            pltpu.VMEM((chips - 1, slab // chips, LANES), jnp.float32),
             pltpu.SemaphoreType.DMA((chunks, n - 1)),
             pltpu.SemaphoreType.DMA((chunks, n - 1)),
             pltpu.SemaphoreType.DMA((chunks,)),
             pltpu.SemaphoreType.DMA((2, 2)),
+            pltpu.SemaphoreType.DMA((2, stages)),
         ],
         compiler_params=pltpu.CompilerParams(
             collective_id=0, has_side_effects=True, vmem_limit_bytes=56 * 2**20
@@ -144,22 +240,44 @@
 
 def inverse_cholesky(cross):
     rank = cross.shape[0]
-    row = lax.broadcasted_iota(jnp.int32, (rank, 1), 0)
+    row = lax.broadcasted_iota(jnp.int32, (rank, 2 * rank), 0)
     here = lax.broadcasted_iota(jnp.int32, (rank, rank), 0)
     there = lax.broadcasted_iota(jnp.int32, (rank, rank), 1)
-    left, right = cross, (here == there).astype(jnp.float32)
-    for k in range(rank - 1):
-        factor = left[:, k : k + 1] / left[k : k + 1, k : k + 1]
-        factor = jnp.where(row > k, factor, 0.0)
-        left = left - factor * left[k : k + 1, :]
-        right = right - factor * right[k : k + 1, :]
-    pivots = jnp.sum(jnp.where(here == there, left, 0.0), axis=1, keepdims=True)
-    return right / jnp.sqrt(pivots)
+    both = jnp.concatenate([cross, (here == there).astype(jnp.float32)], axis=1)
+    scales = []
+    for k in range(0, rank, 8):
+        columns = [
+            jnp.broadcast_to(both[:, k + t : k + t + 1], both.shape) for t in range(8)
+        ]
+        lines = [both[k + t : k + t + 1, :] for t in range(8)]
+        for t in range(8):
+            at = k + t
+            pivot = columns[t][at : at + 1, :]
+            factor = jnp.where(row > at, columns[t] / pivot, 0.0)
+            for u in range(t + 1, 8):
+                columns[u] = columns[u] - factor * columns[t][k + u : k + u + 1, :]
+                lines[u] = lines[u] - factor[k + u : k + u + 1, :] * lines[t]
+            both = both - factor * lines[t]
+            scales.append(pivot)
+    pivots = jnp.concatenate(scales, axis=0)[:, :rank]
+    return both[:, rank:] / jnp.sqrt(pivots)
 
 
 def iterate_kernel(part, start, out):
-    half = part[...]
-    gram = half + half.T
+    tiles = start.shape[1] // LANES
+
+    def tile(i, j):
+        return part[pl.ds(tile_index(i, j) * LANES, LANES)]
+
+    gram = jnp.concatenate(
+        [
+            jnp.concatenate(
+                [tile(i, j) if j <= i else tile(j, i).T for j in range(tiles)], axis=1
+            )
+            for i in range(tiles)
+        ],
+        axis=0,
+    )
     basis = start[...]
     for _ in range(ITERS):
         image = exact(basis, gram)
@@ -201,8 +319,8 @@
     fold = third // LANES
     sub = fold * fourth
     tiles = field.reshape(rows, seconds, fold, LANES, fourth).transpose(0, 1, 2, 4, 3)
-    part, hi, lo = exchange(tiles.reshape(rows, seconds, sub, LANES), n)
-    part = lax.psum(part, ("grp", "dev"))
+    groups = lax.axis_size("grp")
+    part, hi, lo = exchange(tiles.reshape(rows, seconds, sub, LANES), n, groups)
     basis = pl.pallas_call(
         iterate_kernel,
         out_shape=jax.ShapeDtypeStruct((rank, start_basis.shape[0]), jnp.float32),

time: 922 us -> 790 us (0.86)
  waiting for transfers between devices: 130 us -> 0 us
  between operations: 14 us -> 0.66 us
  Pallas kernels: 776 us -> 787 us
    psum x1 -> x0, waiting for transfers between devices: 130 us -> none  [on_device(): part = lax.psum(part, ('grp', 'dev'))]
    pallas_call x1, Pallas kernels: 736 us -> 758 us  [exchange(): pl.pallas_call(functools.partial(exchange_kernel, n, groups), out_shape=(...]
    pallas_call x1, Pallas kernels: 20 us -> 9.55 us  [on_device(): pl.pallas_call(iterate_kernel, out_shape=jax.ShapeDtypeStruct((rank, star...]
  transfers between devices with their start and end apart: 1 -> 0, of which waited for: 1 -> 0; matrix products, arithmetic and copies ran while one was open for 0% -> 0% of each run, Pallas kernels for 0% -> 0%
where the time goes in v2:
time: 790 us
  Pallas kernels  787 us (100%)
    pallas_call x1, Pallas kernels, exchange(): pl.pallas_call(functools.partial(exchange_kernel, n, groups), out_shape=(...  758 us
    pallas_call x1, Pallas kernels, project(): pl.pallas_call(core_kernel, grid=(chunks,), out_shape=jax.ShapeDtypeStruc...  19.7 us

profile of v2, /device:TPU:0, one launch (start us, length us, event | category | flops | bytes accessed | tf_op | source)
XLA Modules:
  0.0 789.9 jit_solution(14080395413386996352)
XLA Ops:
  0.6 0.0 copy-start.2
  0.6 758.0 %shard_map.41 = (f32[1280,128]{1,0:T(8,128)}, bf16[16,512,1024]{2,1,0:T(8,128)(2,1)}, bf16[16,512,1024]{2,1,0:T(8,128)(2,1)}) custom-call(f32[64,128,8,128]{3,2,1,0:T(8,128)} %bitcast.14), custom_call_target="tpu_custom_call" | custom-call | tf_op jit(solution)/shard_map/pallas_call | solution.py:203
  758.7 0.0 copy-done.2
  758.7 0.0 copy-start
  758.7 1.1 copy-done
  759.8 9.6 %shard_map.42.basis = f32[64,512]{1,0:T(8,128)} custom-call(f32[1280,128]{1,0:T(8,128)S(1)} %copy-done, f32[64,512]{1,0:T(8,128)S(1)} %bitcast.13), custom_call_target="tpu_custom_call" | custom-call | tf_op jit(solution)/shard_map/pallas_call | solution.py:324
  769.3 0.0 copy-start.1
  769.3 0.9 copy-done.1
  770.2 19.7 %shard_map.43 = f32[64,16,8,128]{3,2,1,0:T(8,128)} custom-call(f32[64,512]{1,0:T(8,128)S(1)} %copy-done.1, bf16[16,512,1024]{2,1,0:T(8,128)(2,1)} %get-tuple-element.6.hi, bf16[16,512,1024]{2,1,0:T(8,128)(2,1)} %get-tuple-element.7.lo), custom_call_target="tpu_custom_call" | custom-call | tf_op jit(solution)/shard_map/pallas_call | solution.py:305
Async XLA Ops:
  0.6 758.0 %copy-start.2 = (f32[512,64]{0,1:T(8,128)S(1)}, f32[512,64]{0,1:T(8,128)}, u32[]{:S(2)}) copy-start(f32[512,64]{0,1:T(8,128)} %param.3) | copy-start | bytes 393220
  758.7 1.1 copy-start
  769.3 0.9 copy-start.1

commit v3 on v2

--- a/solution.py
+++ b/solution.py
@@ -121,8 +121,12 @@
             field.at[:, me * chunks + c], buf.at[c, pl.ds(me * rows, rows)], own_sem.at[c]
         )
 
-    def start(c):
-        for k in range(n - 1, 0, -1):
+    def start_far(c):
+        for k in range(n - 1, n // 2 - 1, -1):
+            remote(c, k, partner(me, k), me).start()
+
+    def start_near(c):
+        for k in range(n // 2 - 1, 0, -1):
             remote(c, k, partner(me, k), me).start()
         own(c).start()
 
@@ -133,7 +137,11 @@
         )
 
     for c in range(min(WINDOW, chunks)):
-        start(c)
+        start_far(c)
+        if c == 0:
+            start_near(0)
+        if c + 1 < chunks:
+            start_near(c + 1)
     acc[...] = jnp.zeros_like(acc)
 
     def step(c, carry):
@@ -143,7 +151,11 @@
 
         @pl.when(c + WINDOW < chunks)
         def _():
-            start(c + WINDOW)
+            start_far(c + WINDOW)
+
+        @pl.when(c + WINDOW + 1 < chunks)
+        def _():
+            start_near(c + WINDOW + 1)
 
         @pl.when(c >= 2)
         def _():
@@ -179,13 +191,13 @@
         return carry
 
     lax.fori_loop(0, chunks, step, 0)
-    for c in range(max(chunks - 2, 0), chunks):
-        for copy in flush(c, c % 2):
-            copy.wait()
     sum_kernel_stages(
         n, groups, acc, total, (pair_sum, grp_sum), (pair_in, grp_in, chip_in), sum_sem
     )
     part[...] = total[...]
+    for c in range(max(chunks - 2, 0), chunks):
+        for copy in flush(c, c % 2):
+            copy.wait()
 
 
 def exchange(field, n, groups):
@@ -291,23 +303,25 @@
     rank = basis.shape[0]
     high, low = split(basis[...])
     both = jnp.concatenate([high, low], axis=0)
-    first = jnp.dot(both, hi[0], preferred_element_type=jnp.float32)
-    second = jnp.dot(high, lo[0], preferred_element_type=jnp.float32)
-    result = first[:rank] + first[rank:] + second
-    for s in range(sub):
-        out[:, 0, s, :] = result[:, s * LANES : (s + 1) * LANES]
+    for c in range(hi.shape[0]):
+        first = jnp.dot(both, hi[c], preferred_element_type=jnp.float32)
+        second = jnp.dot(high, lo[c], preferred_element_type=jnp.float32)
+        result = first[:rank] + first[rank:] + second
+        for s in range(sub):
+            out[:, c, s, :] = result[:, s * LANES : (s + 1) * LANES]
 
 
 def project(basis, hi, lo, sub):
     chunks, full, wide = hi.shape
     rank = basis.shape[0]
-    block = pl.BlockSpec((1, full, wide), lambda c: (c, 0, 0))
+    together = 2 if chunks % 2 == 0 else 1
+    block = pl.BlockSpec((together, full, wide), lambda c: (c, 0, 0))
     return pl.pallas_call(
         core_kernel,
-        grid=(chunks,),
+        grid=(chunks // together,),
         out_shape=jax.ShapeDtypeStruct((rank, chunks, sub, LANES), jnp.float32),
         in_specs=[pl.BlockSpec((rank, full), lambda c: (0, 0)), block, block],
-        out_specs=pl.BlockSpec((rank, 1, sub, LANES), lambda c: (0, c, 0, 0)),
+        out_specs=pl.BlockSpec((rank, together, sub, LANES), lambda c: (0, c, 0, 0)),
         compiler_params=pltpu.CompilerParams(vmem_limit_bytes=40 * 2**20),
     )(basis, hi, lo)
 

time: 790 us -> 786 us (level)
  no operation moved by 1% of the time
where the time goes in v3:
time: 786 us
  Pallas kernels  783 us (100%)
    pallas_call x1, Pallas kernels, exchange(): pl.pallas_call(functools.partial(exchange_kernel, n, groups), out_shape=(...  758 us
    pallas_call x1, Pallas kernels, project(): pl.pallas_call(core_kernel, grid=(chunks // together,), out_shape=jax.Sha...  16.2 us

profile of v3, /device:TPU:0, one launch (start us, length us, event | category | flops | bytes accessed | tf_op | source)
XLA Modules:
  0.0 786.0 jit_solution(11813240090875190886)
XLA Ops:
  0.6 0.0 copy-start.2
  0.6 757.6 %shard_map.41 = (f32[1280,128]{1,0:T(8,128)}, bf16[16,512,1024]{2,1,0:T(8,128)(2,1)}, bf16[16,512,1024]{2,1,0:T(8,128)(2,1)}) custom-call(f32[64,128,8,128]{3,2,1,0:T(8,128)} %bitcast.14), custom_call_target="tpu_custom_call" | custom-call | tf_op jit(solution)/shard_map/pallas_call | solution.py:215
  758.3 0.0 copy-done.2
  758.3 0.0 copy-start
  758.3 1.1 copy-done
  759.4 9.6 %shard_map.42.basis = f32[64,512]{1,0:T(8,128)} custom-call(f32[1280,128]{1,0:T(8,128)S(1)} %copy-done, f32[64,512]{1,0:T(8,128)S(1)} %bitcast.13), custom_call_target="tpu_custom_call" | custom-call | tf_op jit(solution)/shard_map/pallas_call | solution.py:338
  768.9 0.0 copy-start.1
  768.9 0.9 copy-done.1
  769.9 16.2 %shard_map.43 = f32[64,16,8,128]{3,2,1,0:T(8,128)} custom-call(f32[64,512]{1,0:T(8,128)S(1)} %copy-done.1, bf16[16,512,1024]{2,1,0:T(8,128)(2,1)} %get-tuple-element.6.hi, bf16[16,512,1024]{2,1,0:T(8,128)(2,1)} %get-tuple-element.7.lo), custom_call_target="tpu_custom_call" | custom-call | tf_op jit(solution)/shard_map/pallas_call | solution.py:319
Async XLA Ops:
  0.6 757.7 %copy-start.2 = (f32[512,64]{0,1:T(8,128)S(1)}, f32[512,64]{0,1:T(8,128)}, u32[]{:S(2)}) copy-start(f32[512,64]{0,1:T(8,128)} %param.3) | copy-start | bytes 393220
  758.3 1.1 copy-start
  768.9 0.9 copy-start.1
